TPU v7x, 512 devices: a whole 4x8x8 slice. The times are simulated.
512 devices in a mesh: scen: 32 (over y, z_hi), tile: 16 (over x, z_lo, core).
Axes of the slice: x: 4, y: 8, z: 8 (z_hi: 4, z_lo: 2; z = z_hi * 2 + z_lo), core: 2. Of those that a mesh axis runs over, the one named last changes fastest.
Arguments:
- right_first: float32 [8192, 256], P('tile'), may hold values from -6 to 6
- right_scen: bfloat16 [32, 2048, 256], P('scen', 'tile'), may hold values from -6 to 6
- kkt_inverse: bfloat16 [32, 2048, 2048], P('scen', 'tile')
- border: bfloat16 [32, 2048, 8192], P('scen', None, 'tile'), may hold values from -0.09375 to 0.09375
- block_mask: int32 [32, 64], P('scen', 'tile'), may hold values 0 or 1
- factor_inverse: float32 [8192, 8192], P('scen', 'tile')
Outputs:
- first_sens: float32 [8192, 256], P('tile')
- scen_sens: float32 [32, 2048, 256], P('scen', 'tile')
All inputs are finite; a program needn't handle non-finite values. No bound on the sum of `block_mask` on one device may be relied on, other than what follows from the above.
Results may differ from a plain program's by a relative error of at most 0.0045.
Values may be sent and summed in bfloat16 or wider, within the bound.
A program may use at most 64 MiB of HBM per device.

v0:
```python
import jax
import jax.numpy as jnp
from jax import lax
from jax.sharding import PartitionSpec as P


def per_device(right_first, right_scen, kkt_inverse, border, block_mask, factor_inverse):
    width = border.shape[2] // block_mask.shape[1]
    expanded = jnp.repeat(block_mask.astype(jnp.bfloat16), width, axis=1)
    masked = border * expanded[:, None, :]
    rights = lax.all_gather(right_scen, "tile", axis=1, tiled=True)
    weighted = jnp.einsum("sik,skp->sip", kkt_inverse, rights, preferred_element_type=jnp.float32)
    weighted = weighted.astype(jnp.bfloat16)
    partial_sum = jnp.einsum(
        "skc,skp->cp",
        masked,
        lax.all_gather(weighted, "tile", axis=1, tiled=True),
        preferred_element_type=jnp.float32,
    )
    first_rhs = right_first - lax.psum(partial_sum, "scen")
    half = lax.psum(jnp.dot(factor_inverse, first_rhs, precision=lax.Precision.HIGHEST), "tile")
    first_sens = lax.psum(jnp.dot(factor_inverse.T, half, precision=lax.Precision.HIGHEST), "scen")
    first_half = first_sens.astype(jnp.bfloat16)
    images = lax.psum(
        jnp.einsum("skc,cp->skp", masked, first_half, preferred_element_type=jnp.float32), "tile"
    )
    update = (rights.astype(jnp.float32) - images).astype(jnp.bfloat16)
    scen_sens = jnp.einsum("sik,skp->sip", kkt_inverse, update, preferred_element_type=jnp.float32)
    return (first_sens, scen_sens)


def solution(mesh):
    in_specs = (
        P("tile", None),
        P("scen", "tile", None),
        P("scen", "tile", None),
        P("scen", None, "tile"),
        P("scen", "tile"),
        P("scen", "tile"),
    )
    out_specs = (P("tile", None), P("scen", "tile", None))
    return jax.shard_map(
        per_device, mesh=mesh, in_specs=in_specs, out_specs=out_specs, check_vma=False
    )
```

profile of v0, /device:TPU:1, one launch (start us, length us, event | category | flops | bytes accessed | tf_op | source)
XLA Modules:
  0.0 1006.3 jit_solution(15988736709926071064)
XLA Ops:
  7.2 0.0 all-gather.4.cloned.1.call-start
  7.2 0.7 all-gather.4.cloned.1.call-update
  7.9 0.0 all-gather.6.cloned.1.call-start
  8.0 46.0 %all-gather.4.cloned.1.call-done = bf16[1,2048,256]{2,1,0:T(8,128)(2,1)} async-done(((bf16[1,128,256]{2,1,0:T(8,128)(2,1)}), bf16[1,2048,256]{2,1,0:T(8,128)(2,1)}) %all-gather.4.cloned.1.call-update) | async-done | bytes 1048592 | tf_op jit(solution)/shard_map/all_gather | solution.py:11
  54.0 2.3 convolution_convert_fusion
  56.3 0.0 all-reduce.5.cloned.1.call-start
  56.4 0.7 convert_bitcast_fusion
  57.0 0.1 broadcast_bitcast_fusion
  57.1 37.4 %all-gather.6.cloned.1.call-done = bf16[2048,256]{1,0:T(8,128)(2,1)} async-done(((bf16[128,256]{1,0:T(8,128)(2,1)}), bf16[2048,256]{1,0:T(8,128)(2,1)}) %all-gather.6.cloned.1.call-update) | async-done | bytes 1048592 | tf_op jit(solution)/shard_map/all_gather | solution.py:17
  94.6 3.4 fusion.1
  98.0 0.0 all-reduce.7.cloned.1.call-start
  98.0 296.8 %all-reduce.5.cloned.1.call-done = f32[512,256]{1,0:T(8,128)} async-done(((f32[512,256]{1,0:T(8,128)}), f32[512,256]{1,0:T(8,128)}) %all-reduce.5.cloned.1.call-update) | async-done | bytes 524304 | tf_op jit(solution)/shard_map/psum | solution.py:20
  394.8 2.7 convolution_bitcast_fusion.2
  397.6 0.0 all-reduce.9.cloned.1.call-start
  397.7 143.6 %all-reduce.7.cloned.1.call-done = f32[256,256]{0,1:T(8,128)} async-done(((f32[256,256]{0,1:T(8,128)}), f32[256,256]{0,1:T(8,128)}) %all-reduce.7.cloned.1.call-update) | async-done | bytes 262160 | tf_op jit(solution)/shard_map/psum | solution.py:21
  541.3 2.4 convolution_bitcast_fusion.1
  543.6 0.0 all-reduce.11.cloned.1.call-start
  543.7 298.6 %all-reduce.9.cloned.1.call-done = f32[512,256]{0,1:T(8,128)} async-done(((f32[512,256]{0,1:T(8,128)}), f32[512,256]{0,1:T(8,128)}) %all-reduce.9.cloned.1.call-update) | async-done | bytes 524304 | tf_op jit(solution)/shard_map/psum | solution.py:22
  842.3 3.1 convolution_bitcast_fusion
  845.4 1.0 copy-done.3
  846.5 1.0 copy.8
  847.4 149.1 %all-reduce.11.cloned.1.call-done = f32[1,2048,256]{2,1,0:T(8,128)} async-done(((f32[1,2048,256]{2,1,0:T(8,128)}), f32[1,2048,256]{2,1,0:T(8,128)}) %all-reduce.11.cloned.1.call-update) | async-done | bytes 2097168 | tf_op jit(solution)/shard_map/psum | solution.py:24
  996.6 2.1 convolution_bitcast_fusion.3
  998.7 0.8 copy.9
  (16 shorter events, 0.1 us)
Async XLA Ops:
  7.2 387.7 %copy-start = (f32[256,512]{1,0:T(8,128)S(1)}, f32[256,512]{1,0:T(8,128)}, u32[]{:S(2)}) copy-start(f32[256,512]{1,0:T(8,128)} %param.11) | copy-start | bytes 1572868
  7.2 46.8 %all-gather.4.cloned.1.call-start = ((), (), s32[]{:S(2)}) async-start(), calls=%async_computation | async-start | bytes 1114112 | tf_op jit(solution)/shard_map/all_gather | solution.py:11
  7.9 86.6 %all-gather.6.cloned.1.call-start = ((), (), s32[]{:S(2)}) async-start(), calls=%async_computation.5 | async-start | bytes 1114112 | tf_op jit(solution)/shard_map/all_gather | solution.py:17
  56.3 338.5 %all-reduce.5.cloned.1.call-start = ((), (), s32[]{:S(2)}) async-start(), calls=%async_computation.1 | async-start | bytes 1048576 | tf_op jit(solution)/shard_map/psum | solution.py:20
  57.1 337.7 %copy-start.5 = (f32[512,256]{1,0:T(8,128)S(1)}, f32[512,256]{1,0:T(8,128)}, u32[]{:S(2)}) copy-start(f32[512,256]{1,0:T(8,128)} %param.6) | copy-start | bytes 1572868
  98.0 744.3 %copy-start.2 = (bf16[1,2048,512]{2,1,0:T(8,128)(2,1)S(1)}, bf16[1,2048,512]{2,1,0:T(8,128)(2,1)}, u32[]{:S(2)}) copy-start(bf16[1,2048,512]{2,1,0:T(8,128)(2,1)} %param.9) | copy-start | bytes 6291460
  98.0 443.3 %all-reduce.7.cloned.1.call-start = ((), (), s32[]{:S(2)}) async-start(), calls=%async_computation.2 | async-start | bytes 524288 | tf_op jit(solution)/shard_map/psum | solution.py:21
  397.6 444.7 %all-reduce.9.cloned.1.call-start = ((), (), s32[]{:S(2)}) async-start(), calls=%async_computation.3 | async-start | bytes 1048576 | tf_op jit(solution)/shard_map/psum | solution.py:22
  543.6 453.0 %all-reduce.11.cloned.1.call-start = ((), (), s32[]{:S(2)}) async-start(), calls=%async_computation.4 | async-start | bytes 4194304 | tf_op jit(solution)/shard_map/psum | solution.py:24
  845.4 1.0 copy-start.3
  845.4 151.2 %copy-start.1 = (bf16[1,2048,256]{2,1,0:T(8,128)(2,1)S(1)}, bf16[1,2048,256]{2,1,0:T(8,128)(2,1)}, u32[]{:S(2)}) copy-start(bf16[1,2048,256]{2,1,0:T(8,128)(2,1)} %all-gather.4.cloned.1.call-done) | copy-start | bytes 3145732
  845.4 151.2 %copy-start.4 = (bf16[1,128,2048]{2,1,0:T(8,128)(2,1)S(1)}, bf16[1,128,2048]{2,1,0:T(8,128)(2,1)}, u32[]{:S(2)}) copy-start(bf16[1,128,2048]{2,1,0:T(8,128)(2,1)} %param.8) | copy-start | bytes 1572868
Sparse Core Ops, SparseCore 0:
  10.2 43.7 all-gather.3
  56.7 37.8 all-gather.5
  98.1 296.6 all-reduce.4
  398.4 142.7 all-reduce.6
  544.6 297.6 all-reduce.8
  845.6 150.9 all-reduce.10
where the time goes:
time: 1010 us
  waiting for transfers between devices  972 us (96%)
  matrix products  16 us (2%)
  between operations  14.1 us (1%)
    psum x1, waiting for transfers between devices, per_device(): lax.psum(jnp.dot(factor_inverse.T, half, precision=lax.Precision.HIGHEST)...  299 us
    psum x1, waiting for transfers between devices, per_device(): first_rhs = right_first - lax.psum(partial_sum, 'scen')  297 us
    psum x1, waiting for transfers between devices, per_device(): lax.psum(jnp.einsum('skc,cp->skp', masked, first_half, preferred_element_...  149 us
    psum x1, waiting for transfers between devices, per_device(): lax.psum(jnp.dot(factor_inverse, first_rhs, precision=lax.Precision.HIGHE...  144 us
    all_gather x1, waiting for transfers between devices, per_device(): rights = lax.all_gather(right_scen, 'tile', axis=1, tiled=True)  46 us
    all_gather x1, waiting for transfers between devices, per_device(): lax.all_gather(weighted, 'tile', axis=1, tiled=True)  37.4 us
  transfers between devices with their start and end apart: 6, of which 6 were waited for; matrix products, arithmetic and copies ran while one was open for 0% of the time, Pallas kernels for 0%

commit v1 on v0

v1 whole, which is shorter than its diff:
```python
import jax
import jax.numpy as jnp
from jax import lax
from jax.experimental import pallas as pl
from jax.experimental.pallas import tpu as pltpu
from jax.sharding import PartitionSpec as P

MESH = pl.DeviceIdType.MESH
BF = jnp.bfloat16
F32 = jnp.float32
SCEN, TILE, CHIPS = 32, 16, 8
HALF = 128
Y_ORDER = (4, 3, 5, 2, 6, 1, 7, 0)
Z_ORDER = (2, 1, 3, 0)
SCEN_STEPS = [(dy, dz) for dy in Y_ORDER for dz in Z_ORDER if dy or dz]
CHIP_STEPS = [(2, 1), (1, 1), (3, 1), (2, 0), (1, 0), (3, 0), (0, 1)]


def kernel(
    rf, rs, kinv, bord, mask, fac,
    o1, o2,
    kc, bc, bt, fv, fhi, flo, fthi, ftlo, rfs, mx, mxs,
    ra, wb, pf, psend, cr, rh, hp, dr, hf, er, hh, hm, fs, fr, ug, sv, sr, o1v, o2v, hx,
    loc, ssem, rsem,
):
    s = lax.axis_index("scen")
    t = lax.axis_index("tile")
    q, c = t // 2, t % 2
    x, zl = q // 2, q % 2
    y, zh = s // 4, s % 4
    oc = 1 - c
    sib = (s, q * 2 + oc)

    def chip(dx, dz):
        return ((x + dx) % 4) * 2 + (zl + dz) % 2

    chips = [chip(dx, dz) for dx, dz in CHIP_STEPS]
    scens = [((y + dy) % 8) * 4 + (zh + dz) % 4 for dy, dz in SCEN_STEPS]

    def remote(src, dst, n, dev):
        pltpu.make_async_remote_copy(
            src_ref=src, dst_ref=dst, send_sem=ssem.at[n], recv_sem=rsem.at[n],
            device_id=dev, device_id_type=MESH,
        ).start()

    def arrived(ref, n):
        pltpu.make_async_copy(ref, ref, rsem.at[n]).wait()

    def sent(ref, n):
        pltpu.make_async_copy(ref, ref, ssem.at[n]).wait()

    def rows(i, n):
        return pl.ds(pl.multiple_of(i * n, n), n)

    own = [
        pltpu.make_async_copy(kinv.at[0], kc.at[rows(c, 128)], loc.at[0]),
        pltpu.make_async_copy(bord.at[0], bc.at[c], loc.at[1]),
        pltpu.make_async_copy(fac, fv.at[c], loc.at[2]),
        pltpu.make_async_copy(rf.at[rows(s % 16, 32), rows(c, 128)], rfs.at[c], loc.at[3]),
        pltpu.make_async_copy(rs.at[0, :, rows(c, 128)], ra.at[rows(t, 128)], loc.at[4]),
    ]
    for cp in own:
        cp.start()

    barrier = pltpu.get_barrier_semaphore()
    for p in chips:
        for cc in range(2):
            pl.semaphore_signal(barrier, inc=1, device_id=(s, p * 2 + cc), device_id_type=MESH)
    pl.semaphore_signal(barrier, inc=1, device_id=sib, device_id_type=MESH)
    for p in scens:
        pl.semaphore_signal(barrier, inc=1, device_id=(p, t), device_id_type=MESH)
    pl.semaphore_wait(barrier, TILE - 1 + SCEN - 1)

    for cc in range(2):
        for p in chips:
            remote(rs.at[0, :, rows(cc, 128)], ra.at[rows(t, 128)], 0, (s, p * 2 + cc))
    remote(rs.at[0, :, rows(oc, 128)], ra.at[rows(t, 128)], 0, sib)
    remote(kinv.at[0], kc.at[rows(c, 128)], 1, sib)
    remote(rf.at[rows(s % 16, 32), rows(oc, 128)], rfs.at[c], 2, sib)
    for b in range(4):
        mx[c, pl.ds(b * 8, 8)] = jnp.broadcast_to(mask[0:1, b : b + 1].astype(F32), (8, 128))
    remote(mx.at[c], mx.at[c], 3, sib)
    remote(bord.at[0], bc.at[c], 4, sib)
    remote(fac, fv.at[c], 5, sib)

    own[0].wait()
    own[4].wait()
    arrived(kc.at[rows(oc, 128)], 1)
    arrived(ra.at[pl.ds(0, 15 * 128)], 0)
    for i in range(2):
        r = pl.ds(i * 128, 128)
        w = jnp.dot(kc[r], ra[...], preferred_element_type=F32)
        wb[pl.ds(pl.multiple_of(q * 256 + i * 128, 128), 128)] = w.astype(BF)
    for p in chips:
        remote(wb.at[rows(q, 256)], wb.at[rows(q, 256)], 6, (s, p * 2 + c))

    own[1].wait()
    arrived(bc.at[oc], 4)
    arrived(mx.at[oc], 3)

    @pl.loop(0, 8)
    def _(i):
        for cc in range(2):
            for j in range(2):
                blk = bc[cc, rows(i, 256), pl.ds(j * 256, 256)]
                bt[pl.ds(cc * 512 + j * 256, 256), rows(i, 256)] = blk.T

    arrived(wb.at[pl.ds(0, 7 * 256)], 6)
    for k in range(4):
        r = (s // 8 + k) % 4
        p = jnp.dot(bt[rows(r, 256)], wb[...], preferred_element_type=F32)
        for j in range(2):
            keep = mx[r // 2, pl.ds(pl.multiple_of((r % 2) * 16 + j * 8, 8), 1)]
            v = jnp.where(keep > 0.5, p[j * 128 : (j + 1) * 128], 0.0)
            psend[pl.ds(r * 8 + j * 4, 4)] = v.astype(BF).reshape(4, 32, 128)
        for j in range(8):
            d = r * 8 + (s % 8 + j) % 8

            @pl.when(d != s)
            def _():
                remote(psend.at[d], cr.at[s], 7, (d, t))

    own[2].wait()
    arrived(fv.at[oc], 5)
    for cc in range(2):
        for j in range(2):
            v = fv[cc, :, pl.ds(j * 256, 256)]
            hi = v.astype(BF)
            lo = (v - hi.astype(F32)).astype(BF)
            at = pl.ds(cc * 512 + j * 256, 256)
            fhi[:, at] = hi
            flo[:, at] = lo
            fthi[at] = hi.T
            ftlo[at] = lo.T
    own[3].wait()
    arrived(rfs.at[oc], 2)
    cr[s] = psend[s]
    arrived(psend.at[pl.ds(0, 31)], 7)
    total = cr[0].astype(F32)
    for i in range(1, SCEN):
        total += cr[i].astype(F32)
    rh[rows(s, 32)] = (rfs[s // 16] - total).astype(BF)
    for p in scens:
        remote(rh.at[rows(s, 32)], rh.at[rows(s, 32)], 8, (p, t))
    arrived(rh.at[pl.ds(0, 31 * 32)], 8)

    for i in range(2):
        r = pl.ds(i * 128, 128)
        h = jnp.dot(fhi[r], rh[...], preferred_element_type=F32)
        h += jnp.dot(flo[r], rh[...], preferred_element_type=F32)
        hp[pl.ds(i * 4, 4)] = h.reshape(4, 32, 128)
    for p in chips:
        remote(hp.at[p], dr.at[q], 9, (s, p * 2 + c))
    dr[q] = hp[q]
    arrived(dr.at[pl.ds(0, 7)], 9)
    total = dr[0]
    for i in range(1, CHIPS):
        total += dr[i]
    hf[q] = total
    for p in chips:
        remote(hf.at[q], hf.at[q], 10, (s, p * 2 + c))
    arrived(hf.at[pl.ds(0, 7)], 10)

    half = hf[...].reshape(256, HALF)
    hhi = half.astype(BF)
    hlo = (half - hhi.astype(F32)).astype(BF)
    for k in range(4):
        r = (s // 8 + k) % 4
        v = jnp.dot(fthi[rows(r, 256)], hhi, preferred_element_type=F32)
        v += jnp.dot(fthi[rows(r, 256)], hlo, preferred_element_type=F32)
        v += jnp.dot(ftlo[rows(r, 256)], hhi, preferred_element_type=F32)
        pf[pl.ds(r * 8, 8)] = v.astype(BF).reshape(8, 32, 128)
        for j in range(8):
            d = r * 8 + (s % 8 + j) % 8

            @pl.when(d != s)
            def _():
                remote(pf.at[d], er.at[s], 11, (d, t))

    er[s] = pf[s]
    arrived(pf.at[pl.ds(0, 31)], 11)
    total = er[0].astype(F32)
    for i in range(1, SCEN):
        total += er[i].astype(F32)
    hh[rows(s, 32)] = total.astype(BF)
    for p in scens:
        remote(hh.at[rows(s, 32)], hh.at[rows(s, 32)], 12, (p, t))
    arrived(hh.at[pl.ds(0, 31 * 32)], 12)

    remote(hh.at[rows(oc, 512)], hx.at[pl.ds(0, 512)], 13, sib)
    for b in range(8):
        keep = mx[b // 4, pl.ds((b % 4) * 8, 1)]
        v = hh[pl.ds(b * 128, 128)].astype(F32)
        hm[pl.ds(b * 128, 128)] = jnp.where(keep > 0.5, v, 0.0).astype(BF)
    for p in [*chips, q]:
        at = rows(p, 256)
        v = jnp.dot(bc[0, at], hm[pl.ds(0, 512)], preferred_element_type=F32)
        v += jnp.dot(bc[1, at], hm[pl.ds(512, 512)], preferred_element_type=F32)
        fs[p] = v.astype(BF)
        if p is not q:
            remote(fs.at[p], fr.at[q], 14, (s, p * 2 + c))
    fr[q] = fs[q]

    arrived(hx, 13)
    o1v[:, rows(c, 128)] = hh[rows(c, 512)].astype(F32)
    o1v[:, rows(oc, 128)] = hx[...].astype(F32)
    out1 = pltpu.make_async_copy(o1v, o1, loc.at[5])
    out1.start()

    arrived(fs.at[pl.ds(0, 7)], 14)
    total = fr[0].astype(F32)
    for i in range(1, CHIPS):
        total += fr[i].astype(F32)
    ug[rows(q, 256)] = (ra[rows(q, 256)].astype(F32) - total).astype(BF)
    for p in chips:
        remote(ug.at[rows(q, 256)], ug.at[rows(q, 256)], 15, (s, p * 2 + c))
    arrived(ug.at[pl.ds(0, 7 * 256)], 15)
    sv[...] = jnp.dot(kc[rows(oc, 128)], ug[...], preferred_element_type=F32)
    remote(sv, sr, 16, sib)
    o2v[:, rows(c, 128)] = jnp.dot(kc[rows(c, 128)], ug[...], preferred_element_type=F32)
    arrived(sr, 16)
    o2v[:, rows(oc, 128)] = sr[...]
    out2 = pltpu.make_async_copy(o2v, o2.at[0], loc.at[6])
    out2.start()

    sent(ra.at[pl.ds(0, 15 * 128)], 0)
    sent(kc.at[rows(c, 128)], 1)
    sent(rfs.at[c], 2)
    sent(mx.at[c], 3)
    sent(bc.at[c], 4)
    sent(fv.at[c], 5)
    sent(wb.at[pl.ds(0, 7 * 256)], 6)
    sent(psend.at[pl.ds(0, 31)], 7)
    sent(rh.at[pl.ds(0, 31 * 32)], 8)
    sent(hp.at[pl.ds(0, 7)], 9)
    sent(hf.at[pl.ds(0, 7)], 10)
    sent(pf.at[pl.ds(0, 31)], 11)
    sent(hh.at[pl.ds(0, 31 * 32)], 12)
    sent(hx, 13)
    sent(fs.at[pl.ds(0, 7)], 14)
    sent(ug.at[pl.ds(0, 7 * 256)], 15)
    sent(sv, 16)
    out1.wait()
    out2.wait()


def per_device(right_first, right_scen, kkt_inverse, border, block_mask, factor_inverse):
    hbm = pl.BlockSpec(memory_space=pl.ANY)
    return pl.pallas_call(
        kernel,
        out_shape=(
            jax.ShapeDtypeStruct((512, 256), F32),
            jax.ShapeDtypeStruct((1, 128, 256), F32),
        ),
        in_specs=[hbm, hbm, hbm, hbm, pl.BlockSpec(memory_space=pltpu.VMEM), hbm],
        out_specs=(hbm, hbm),
        scratch_shapes=[
            pltpu.VMEM((256, 2048), BF),
            pltpu.VMEM((2, 2048, 512), BF),
            pltpu.VMEM((1024, 2048), BF),
            pltpu.VMEM((2, 256, 512), F32),
            pltpu.VMEM((256, 1024), BF),
            pltpu.VMEM((256, 1024), BF),
            pltpu.VMEM((1024, 256), BF),
            pltpu.VMEM((1024, 256), BF),
            pltpu.VMEM((2, 32, 128), F32),
            pltpu.VMEM((2, 32, 128), F32),
            pltpu.VMEM((8, 128), F32),
            pltpu.VMEM((2048, 128), BF),
            pltpu.VMEM((2048, 128), BF),
            pltpu.VMEM((32, 32, 128), BF),
            pltpu.VMEM((32, 32, 128), BF),
            pltpu.VMEM((32, 32, 128), BF),
            pltpu.VMEM((1024, 128), BF),
            pltpu.VMEM((8, 32, 128), F32),
            pltpu.VMEM((8, 32, 128), F32),
            pltpu.VMEM((8, 32, 128), F32),
            pltpu.VMEM((32, 32, 128), BF),
            pltpu.VMEM((1024, 128), BF),
            pltpu.VMEM((1024, 128), BF),
            pltpu.VMEM((8, 256, 128), BF),
            pltpu.VMEM((8, 256, 128), BF),
            pltpu.VMEM((2048, 128), BF),
            pltpu.VMEM((128, 128), F32),
            pltpu.VMEM((128, 128), F32),
            pltpu.VMEM((512, 256), F32),
            pltpu.VMEM((128, 256), F32),
            pltpu.VMEM((512, 128), BF),
            pltpu.SemaphoreType.DMA((7,)),
            pltpu.SemaphoreType.DMA((17,)),
            pltpu.SemaphoreType.DMA((17,)),
        ],
        compiler_params=pltpu.CompilerParams(
            collective_id=0, has_side_effects=True, vmem_limit_bytes=48 << 20
        ),
        cost_estimate=pl.CostEstimate(flops=3 * 10**9, bytes_accessed=8 << 20, transcendentals=0),
    )(right_first, right_scen, kkt_inverse, border, block_mask, factor_inverse)


def solution(mesh):
    in_specs = (
        P("tile", None),
        P("scen", "tile", None),
        P("scen", "tile", None),
        P("scen", None, "tile"),
        P("scen", "tile"),
        P("scen", "tile"),
    )
    out_specs = (P("tile", None), P("scen", "tile", None))
    return jax.shard_map(
        per_device, mesh=mesh, in_specs=in_specs, out_specs=out_specs, check_vma=False
    )
```

time: 1010 us -> 108 us (0.11)
  waiting for transfers between devices: 972 us -> 0 us
  Pallas kernels: 0 us -> 99.5 us
  matrix products: 16 us -> 0 us
  between operations: 14.1 us -> 0.65 us
    psum x4 -> x0, waiting for transfers between devices: 888 us -> none  [the longest x1 299 us: per_device(): lax.psum(jnp.dot(factor_inverse.T, half, precision=lax.Precision.HIGHEST)...]
    pallas_call x0 -> x1, Pallas kernels: none -> 99.5 us  [per_device(): pl.pallas_call(kernel, out_shape=(jax.ShapeDtypeStruct((512, 256), F32),...]
    all_gather x2 -> x0, waiting for transfers between devices: 83.5 us -> none  [the longest x1 46 us: per_device(): rights = lax.all_gather(right_scen, 'tile', axis=1, tiled=True)]
    dot_general x6 -> x0, matrix products: 16 us -> none  [the longest x1 3.39 us: per_device(): jnp.einsum('skc,skp->cp', masked, lax.all_gather(weighted, 'tile', axis=1...]
  transfers between devices with their start and end apart: 6 -> 0, of which waited for: 6 -> 0; matrix products, arithmetic and copies ran while one was open for 0% -> 0% of each run, Pallas kernels for 0% -> 0%
where the time goes in v1:
time: 108 us
  Pallas kernels  99.5 us (92%)
  local copies, waits for them, and re-layouts  7.65 us (7%)
    pallas_call x1, Pallas kernels, per_device(): pl.pallas_call(kernel, out_shape=(jax.ShapeDtypeStruct((512, 256), F32),...  99.5 us
    unnamed x14, local copies, waits for them, and re-layouts  7.65 us

profile of v1, /device:TPU:1, one launch (start us, length us, event | category | flops | bytes accessed | tf_op | source)
XLA Modules:
  0.0 107.8 jit_solution(10480755374704612226)
XLA Ops:
  0.6 0.0 copy-start
  0.6 1.6 %copy-done = bf16[1,2048,512]{2,1,0:T(8,128)(2,1)S(1)} copy-done((bf16[1,2048,512]{2,1,0:T(8,128)(2,1)S(1)}, bf16[1,2048,512]{2,1,0:T(8,128)(2,1)}, u32[]{:S(2)}) %copy-start) | copy-done | bytes 2097176
  2.2 0.0 copy-start.1
  2.2 1.0 copy-done.1
  3.3 0.0 copy-start.2
  3.3 1.0 copy-done.2
  4.3 0.0 copy-start.3
  4.3 1.0 copy-done.3
  5.3 0.0 copy-start.4
  5.4 0.8 copy-done.4
  6.2 0.0 copy-start.5
  6.2 0.7 copy-done.5
  6.8 99.5 %shard_map.77 = (f32[512,256]{1,0:T(8,128)S(1)}, f32[1,128,256]{2,1,0:T(8,128)S(1)}) custom-call(f32[512,256]{1,0:T(8,128)S(1)} %copy-done.1, bf16[1,128,256]{2,1,0:T(8,128)(2,1)S(1)} %copy-done.4, bf16[1,128,2048]{2,1,0:T(8,128)(2,1)S(1)} %copy-done.2, bf16[1,2048,512]{2,1,0:T(8,128)(2,1)S(1)} %copy-done, s32[1,4]{1,0:T(1,128)S(1)} %copy-done.5, ...), custom_call_target="tpu_custom_call" | custom-call | flops 3000000000 | bytes 8388608 | tf_op jit(solution)/shard_map/pallas_call | solution.py:249
  106.3 0.8 copy.10
  107.1 0.7 copy.11
Async XLA Ops:
  0.6 1.6 %copy-start = (bf16[1,2048,512]{2,1,0:T(8,128)(2,1)S(1)}, bf16[1,2048,512]{2,1,0:T(8,128)(2,1)}, u32[]{:S(2)}) copy-start(bf16[1,2048,512]{2,1,0:T(8,128)(2,1)} %bord.1) | copy-start | bytes 6291460
  2.2 1.0 copy-start.1
  3.3 1.0 copy-start.2
  4.3 1.0 copy-start.3
  5.3 0.8 copy-start.4
  6.2 0.7 copy-start.5

commit v2 on v1

--- a/solution.py
+++ b/solution.py
@@ -19,9 +19,9 @@
 def kernel(
     rf, rs, kinv, bord, mask, fac,
     o1, o2,
-    kc, bc, bt, fv, fhi, flo, fthi, ftlo, rfs, mx, mxs,
-    ra, wb, pf, psend, cr, rh, hp, dr, hf, er, hh, hm, fs, fr, ug, sv, sr, o1v, o2v, hx,
-    loc, ssem, rsem,
+    kc, bc, bt, fv, fhi, flo, fthi, ftlo, rfs, mx,
+    ra, wb, pf, psend, cr, rh, hp, dr, hf, er, hh, hm, fs, fr, ug, sv, o1v, o2v, hx,
+    pacc, loc, ssem, rsem, ra_sem, wb_sem, rh_sem, ug_sem,
 ):
     s = lax.axis_index("scen")
     t = lax.axis_index("tile")
@@ -37,14 +37,21 @@
     chips = [chip(dx, dz) for dx, dz in CHIP_STEPS]
     scens = [((y + dy) % 8) * 4 + (zh + dz) % 4 for dy, dz in SCEN_STEPS]
 
-    def remote(src, dst, n, dev):
+    def remote(src, dst, n, dev, landed=None):
         pltpu.make_async_remote_copy(
-            src_ref=src, dst_ref=dst, send_sem=ssem.at[n], recv_sem=rsem.at[n],
+            src_ref=src, dst_ref=dst, send_sem=ssem.at[n],
+            recv_sem=rsem.at[n] if landed is None else landed,
             device_id=dev, device_id_type=MESH,
         ).start()
 
     def arrived(ref, n):
         pltpu.make_async_copy(ref, ref, rsem.at[n]).wait()
+
+    def landed(ref, sem):
+        pltpu.make_async_copy(ref, ref, sem).wait()
+
+    near = [q, *reversed(chips)]
+    near_y = [(y + dy) % 8 for dy in reversed(Y_ORDER)]
 
     def sent(ref, n):
         pltpu.make_async_copy(ref, ref, ssem.at[n]).wait()
@@ -71,10 +78,10 @@
         pl.semaphore_signal(barrier, inc=1, device_id=(p, t), device_id_type=MESH)
     pl.semaphore_wait(barrier, TILE - 1 + SCEN - 1)
 
-    for cc in range(2):
+    for cc in (1, 0):
         for p in chips:
-            remote(rs.at[0, :, rows(cc, 128)], ra.at[rows(t, 128)], 0, (s, p * 2 + cc))
-    remote(rs.at[0, :, rows(oc, 128)], ra.at[rows(t, 128)], 0, sib)
+            remote(rs.at[0, :, rows(cc, 128)], ra.at[rows(t, 128)], 0, (s, p * 2 + cc), ra_sem.at[q])
+    remote(rs.at[0, :, rows(oc, 128)], ra.at[rows(t, 128)], 0, sib, ra_sem.at[q])
     remote(kinv.at[0], kc.at[rows(c, 128)], 1, sib)
     remote(rf.at[rows(s % 16, 32), rows(oc, 128)], rfs.at[c], 2, sib)
     for b in range(4):
@@ -86,13 +93,16 @@
     own[0].wait()
     own[4].wait()
     arrived(kc.at[rows(oc, 128)], 1)
-    arrived(ra.at[pl.ds(0, 15 * 128)], 0)
+    w = [jnp.zeros((128, HALF), F32)] * 2
+    for p in near:
+        landed(ra.at[rows(t, 128)] if p is q else ra.at[rows(p, 256)], ra_sem.at[p])
+        for i in range(2):
+            left = kc[pl.ds(i * 128, 128), rows(p, 256)]
+            w[i] += jnp.dot(left, ra[rows(p, 256)], preferred_element_type=F32)
     for i in range(2):
-        r = pl.ds(i * 128, 128)
-        w = jnp.dot(kc[r], ra[...], preferred_element_type=F32)
-        wb[pl.ds(pl.multiple_of(q * 256 + i * 128, 128), 128)] = w.astype(BF)
-    for p in chips:
-        remote(wb.at[rows(q, 256)], wb.at[rows(q, 256)], 6, (s, p * 2 + c))
+        wb[pl.ds(pl.multiple_of(q * 256 + i * 128, 128), 128)] = w[i].astype(BF)
+    for p in chips:
+        remote(wb.at[rows(q, 256)], wb.at[rows(q, 256)], 6, (s, p * 2 + c), wb_sem.at[q])
 
     own[1].wait()
     arrived(bc.at[oc], 4)
@@ -105,10 +115,23 @@
                 blk = bc[cc, rows(i, 256), pl.ds(j * 256, 256)]
                 bt[pl.ds(cc * 512 + j * 256, 256), rows(i, 256)] = blk.T
 
-    arrived(wb.at[pl.ds(0, 7 * 256)], 6)
+    for n, b in enumerate(near[:-1]):
+        if b is not q:
+            landed(wb.at[rows(b, 256)], wb_sem.at[b])
+
+        @pl.loop(0, 4)
+        def _(r):
+            p = jnp.dot(bt[rows(r, 256), rows(b, 256)], wb[rows(b, 256)], preferred_element_type=F32)
+            if n:
+                p += pacc[rows(r, 256)]
+            pacc[rows(r, 256)] = p
+
+    b = near[-1]
+    landed(wb.at[rows(b, 256)], wb_sem.at[b])
     for k in range(4):
         r = (s // 8 + k) % 4
-        p = jnp.dot(bt[rows(r, 256)], wb[...], preferred_element_type=F32)
+        p = jnp.dot(bt[rows(r, 256), rows(b, 256)], wb[rows(b, 256)], preferred_element_type=F32)
+        p += pacc[rows(r, 256)]
         for j in range(2):
             keep = mx[r // 2, pl.ds(pl.multiple_of((r % 2) * 16 + j * 8, 8), 1)]
             v = jnp.where(keep > 0.5, p[j * 128 : (j + 1) * 128], 0.0)
@@ -141,14 +164,16 @@
         total += cr[i].astype(F32)
     rh[rows(s, 32)] = (rfs[s // 16] - total).astype(BF)
     for p in scens:
-        remote(rh.at[rows(s, 32)], rh.at[rows(s, 32)], 8, (p, t))
-    arrived(rh.at[pl.ds(0, 31 * 32)], 8)
-
+        remote(rh.at[rows(s, 32)], rh.at[rows(s, 32)], 8, (p, t), rh_sem.at[y])
+    h = [jnp.zeros((128, HALF), F32)] * 2
+    for n, p in enumerate(near_y):
+        landed(rh.at[pl.ds(0, 128 if n else 96)], rh_sem.at[p])
+        for i in range(2):
+            r = pl.ds(i * 128, 128)
+            for part in (fhi, flo):
+                h[i] += jnp.dot(part[r, rows(p, 128)], rh[rows(p, 128)], preferred_element_type=F32)
     for i in range(2):
-        r = pl.ds(i * 128, 128)
-        h = jnp.dot(fhi[r], rh[...], preferred_element_type=F32)
-        h += jnp.dot(flo[r], rh[...], preferred_element_type=F32)
-        hp[pl.ds(i * 4, 4)] = h.reshape(4, 32, 128)
+        hp[pl.ds(i * 4, 4)] = h[i].reshape(4, 32, 128)
     for p in chips:
         remote(hp.at[p], dr.at[q], 9, (s, p * 2 + c))
     dr[q] = hp[q]
@@ -213,15 +238,20 @@
         total += fr[i].astype(F32)
     ug[rows(q, 256)] = (ra[rows(q, 256)].astype(F32) - total).astype(BF)
     for p in chips:
-        remote(ug.at[rows(q, 256)], ug.at[rows(q, 256)], 15, (s, p * 2 + c))
-    arrived(ug.at[pl.ds(0, 7 * 256)], 15)
-    sv[...] = jnp.dot(kc[rows(oc, 128)], ug[...], preferred_element_type=F32)
-    remote(sv, sr, 16, sib)
-    o2v[:, rows(c, 128)] = jnp.dot(kc[rows(c, 128)], ug[...], preferred_element_type=F32)
-    arrived(sr, 16)
-    o2v[:, rows(oc, 128)] = sr[...]
-    out2 = pltpu.make_async_copy(o2v, o2.at[0], loc.at[6])
+        remote(ug.at[rows(q, 256)], ug.at[rows(q, 256)], 15, (s, p * 2 + c), ug_sem.at[q])
+    v = [jnp.zeros((128, HALF), F32)] * 2
+    for p in near:
+        if p is not q:
+            landed(ug.at[rows(p, 256)], ug_sem.at[p])
+        for i, cc in enumerate((oc, c)):
+            left = kc[rows(cc, 128), rows(p, 256)]
+            v[i] += jnp.dot(left, ug[rows(p, 256)], preferred_element_type=F32)
+    sv[...] = v[0]
+    remote(sv, o2.at[0, :, rows(c, 128)], 16, sib)
+    o2v[...] = v[1]
+    out2 = pltpu.make_async_copy(o2v, o2.at[0, :, rows(c, 128)], loc.at[6])
     out2.start()
+    arrived(sv, 16)
 
     sent(ra.at[pl.ds(0, 15 * 128)], 0)
     sent(kc.at[rows(c, 128)], 1)
@@ -265,7 +295,6 @@
             pltpu.VMEM((1024, 256), BF),
             pltpu.VMEM((2, 32, 128), F32),
             pltpu.VMEM((2, 32, 128), F32),
-            pltpu.VMEM((8, 128), F32),
             pltpu.VMEM((2048, 128), BF),
             pltpu.VMEM((2048, 128), BF),
             pltpu.VMEM((32, 32, 128), BF),
@@ -282,16 +311,17 @@
             pltpu.VMEM((8, 256, 128), BF),
             pltpu.VMEM((2048, 128), BF),
             pltpu.VMEM((128, 128), F32),
+            pltpu.VMEM((512, 256), F32),
             pltpu.VMEM((128, 128), F32),
-            pltpu.VMEM((512, 256), F32),
-            pltpu.VMEM((128, 256), F32),
             pltpu.VMEM((512, 128), BF),
+            pltpu.VMEM((1024, 128), F32),
             pltpu.SemaphoreType.DMA((7,)),
             pltpu.SemaphoreType.DMA((17,)),
             pltpu.SemaphoreType.DMA((17,)),
+            *[pltpu.SemaphoreType.DMA((8,))] * 4,
         ],
         compiler_params=pltpu.CompilerParams(
-            collective_id=0, has_side_effects=True, vmem_limit_bytes=48 << 20
+            collective_id=0, has_side_effects=True, vmem_limit_bytes=62 << 20
         ),
         cost_estimate=pl.CostEstimate(flops=3 * 10**9, bytes_accessed=8 << 20, transcendentals=0),
     )(right_first, right_scen, kkt_inverse, border, block_mask, factor_inverse)

time: 108 us -> 107 us (level)
  local copies, waits for them, and re-layouts: 7.65 us -> 3.44 us
  Pallas kernels: 99.5 us -> 103 us
    unnamed x14 -> x2, local copies, waits for them, and re-layouts: 7.65 us -> 3.44 us
    pallas_call x1, Pallas kernels: 99.5 us -> 103 us  [per_device(): pl.pallas_call(kernel, out_shape=(jax.ShapeDtypeStruct((512, 256), F32),...]
where the time goes in v2:
time: 107 us
  Pallas kernels  103 us (96%)
  local copies, waits for them, and re-layouts  3.44 us (3%)
    pallas_call x1, Pallas kernels, per_device(): pl.pallas_call(kernel, out_shape=(jax.ShapeDtypeStruct((512, 256), F32),...  103 us
    unnamed x2, local copies, waits for them, and re-layouts  3.44 us

profile of v2, /device:TPU:1, one launch (start us, length us, event | category | flops | bytes accessed | tf_op | source)
XLA Modules:
  0.0 106.9 jit_solution(6002433239095470255)
XLA Ops:
  0.6 102.8 %shard_map.77 = (f32[512,256]{1,0:T(8,128)}, f32[1,128,256]{2,1,0:T(8,128)}) custom-call(f32[512,256]{1,0:T(8,128)} %rf.1, bf16[1,128,256]{2,1,0:T(8,128)(2,1)} %rs.1, bf16[1,128,2048]{2,1,0:T(8,128)(2,1)} %kinv.1, bf16[1,2048,512]{2,1,0:T(8,128)(2,1)} %bord.1, s32[1,4]{1,0:T(1,128)} %mask.1, f32[256,512]{1,0:T(8,128)} %fac.1), custom_call_target="tpu_custom_call" | custom-call | flops 3000000000 | bytes 8388608 | tf_op jit(solution)/shard_map/pallas_call | solution.py:279
  103.4 1.9 %copy.10 = f32[512,256]{1,0:T(8,128)} copy(f32[512,256]{1,0:T(8,128)} %get-tuple-element.4) | data formatting | bytes 1048576
  105.3 1.6 %copy.11 = f32[1,128,256]{2,1,0:T(8,128)} copy(f32[1,128,256]{2,1,0:T(8,128)} %get-tuple-element.5) | data formatting | bytes 262144

commit v3 on v1

--- a/solution.py
+++ b/solution.py
@@ -19,8 +19,8 @@
 def kernel(
     rf, rs, kinv, bord, mask, fac,
     o1, o2,
-    kc, bc, bt, fv, fhi, flo, fthi, ftlo, rfs, mx, mxs,
-    ra, wb, pf, psend, cr, rh, hp, dr, hf, er, hh, hm, fs, fr, ug, sv, sr, o1v, o2v, hx,
+    kc, bc, bt, fv, fhi, flo, fthi, ftlo, rfs, mx,
+    ra, wb, pf, psend, cr, rh, hp, dr, hf, er, hh, hm, fs, fr, ug, sv, o1v, o2v, hx,
     loc, ssem, rsem,
 ):
     s = lax.axis_index("scen")
@@ -71,7 +71,7 @@
         pl.semaphore_signal(barrier, inc=1, device_id=(p, t), device_id_type=MESH)
     pl.semaphore_wait(barrier, TILE - 1 + SCEN - 1)
 
-    for cc in range(2):
+    for cc in (1, 0):
         for p in chips:
             remote(rs.at[0, :, rows(cc, 128)], ra.at[rows(t, 128)], 0, (s, p * 2 + cc))
     remote(rs.at[0, :, rows(oc, 128)], ra.at[rows(t, 128)], 0, sib)
@@ -216,12 +216,11 @@
         remote(ug.at[rows(q, 256)], ug.at[rows(q, 256)], 15, (s, p * 2 + c))
     arrived(ug.at[pl.ds(0, 7 * 256)], 15)
     sv[...] = jnp.dot(kc[rows(oc, 128)], ug[...], preferred_element_type=F32)
-    remote(sv, sr, 16, sib)
-    o2v[:, rows(c, 128)] = jnp.dot(kc[rows(c, 128)], ug[...], preferred_element_type=F32)
-    arrived(sr, 16)
-    o2v[:, rows(oc, 128)] = sr[...]
-    out2 = pltpu.make_async_copy(o2v, o2.at[0], loc.at[6])
+    remote(sv, o2.at[0, :, rows(c, 128)], 16, sib)
+    o2v[...] = jnp.dot(kc[rows(c, 128)], ug[...], preferred_element_type=F32)
+    out2 = pltpu.make_async_copy(o2v, o2.at[0, :, rows(c, 128)], loc.at[6])
     out2.start()
+    arrived(sv, 16)
 
     sent(ra.at[pl.ds(0, 15 * 128)], 0)
     sent(kc.at[rows(c, 128)], 1)
@@ -265,7 +264,6 @@
             pltpu.VMEM((1024, 256), BF),
             pltpu.VMEM((2, 32, 128), F32),
             pltpu.VMEM((2, 32, 128), F32),
-            pltpu.VMEM((8, 128), F32),
             pltpu.VMEM((2048, 128), BF),
             pltpu.VMEM((2048, 128), BF),
             pltpu.VMEM((32, 32, 128), BF),
@@ -282,16 +280,15 @@
             pltpu.VMEM((8, 256, 128), BF),
             pltpu.VMEM((2048, 128), BF),
             pltpu.VMEM((128, 128), F32),
+            pltpu.VMEM((512, 256), F32),
             pltpu.VMEM((128, 128), F32),
-            pltpu.VMEM((512, 256), F32),
-            pltpu.VMEM((128, 256), F32),
             pltpu.VMEM((512, 128), BF),
             pltpu.SemaphoreType.DMA((7,)),
             pltpu.SemaphoreType.DMA((17,)),
             pltpu.SemaphoreType.DMA((17,)),
         ],
         compiler_params=pltpu.CompilerParams(
-            collective_id=0, has_side_effects=True, vmem_limit_bytes=48 << 20
+            collective_id=0, has_side_effects=True, vmem_limit_bytes=53 << 20
         ),
         cost_estimate=pl.CostEstimate(flops=3 * 10**9, bytes_accessed=8 << 20, transcendentals=0),
     )(right_first, right_scen, kkt_inverse, border, block_mask, factor_inverse)

time: 108 us -> 101 us (0.935)
  local copies, waits for them, and re-layouts: 7.65 us -> 2.94 us
  Pallas kernels: 99.5 us -> 97.2 us
    unnamed x14 -> x6, local copies, waits for them, and re-layouts: 7.65 us -> 2.94 us
    pallas_call x1, Pallas kernels: 99.5 us -> 97.2 us  [per_device(): pl.pallas_call(kernel, out_shape=(jax.ShapeDtypeStruct((512, 256), F32),...]
where the time goes in v3:
time: 101 us
  Pallas kernels  97.2 us (96%)
  local copies, waits for them, and re-layouts  2.94 us (3%)
    pallas_call x1, Pallas kernels, per_device(): pl.pallas_call(kernel, out_shape=(jax.ShapeDtypeStruct((512, 256), F32),...  97.2 us
    unnamed x6, local copies, waits for them, and re-layouts  2.94 us

profile of v3, /device:TPU:1, one launch (start us, length us, event | category | flops | bytes accessed | tf_op | source)
XLA Modules:
  0.0 100.8 jit_solution(4558485864461907886)
XLA Ops:
  0.6 0.0 copy-start
  0.6 0.8 copy-done
  1.5 0.0 copy-start.1
  1.5 0.7 copy-done.1
  2.1 97.2 %shard_map.77 = (f32[512,256]{1,0:T(8,128)S(1)}, f32[1,128,256]{2,1,0:T(8,128)S(1)}) custom-call(f32[512,256]{1,0:T(8,128)} %rf.1, bf16[1,128,256]{2,1,0:T(8,128)(2,1)S(1)} %copy-done, bf16[1,128,2048]{2,1,0:T(8,128)(2,1)} %kinv.1, bf16[1,2048,512]{2,1,0:T(8,128)(2,1)} %bord.1, s32[1,4]{1,0:T(1,128)S(1)} %copy-done.1, f32[256,512]{1,0:T(8,128)} %fac.1), custom_call_target="tpu_custom_call" | custom-call | flops 3000000000 | bytes 8388608 | tf_op jit(solution)/shard_map/pallas_call | solution.py:248
  99.3 0.8 copy.10
  100.1 0.7 copy.11
Async XLA Ops:
  0.6 0.8 copy-start
  1.5 0.7 copy-start.1

commit v4 on v3

--- a/solution.py
+++ b/solution.py
@@ -20,7 +20,7 @@
     rf, rs, kinv, bord, mask, fac,
     o1, o2,
     kc, bc, bt, fv, fhi, flo, fthi, ftlo, rfs, mx,
-    ra, wb, pf, psend, cr, rh, hp, dr, hf, er, hh, hm, fs, fr, ug, sv, o1v, o2v, hx,
+    ra, r2, wb, pf, psend, cr, rh, hp, dr, hf, er, hh, hm, fs, fr, ug, sv, o1v, o2v, hx,
     loc, ssem, rsem,
 ):
     s = lax.axis_index("scen")
@@ -58,6 +58,7 @@
         pltpu.make_async_copy(fac, fv.at[c], loc.at[2]),
         pltpu.make_async_copy(rf.at[rows(s % 16, 32), rows(c, 128)], rfs.at[c], loc.at[3]),
         pltpu.make_async_copy(rs.at[0, :, rows(c, 128)], ra.at[rows(t, 128)], loc.at[4]),
+        pltpu.make_async_copy(rs.at[0, :, rows(oc, 128)], r2.at[rows(c, 128)], loc.at[7]),
     ]
     for cp in own:
         cp.start()
@@ -82,6 +83,7 @@
     remote(mx.at[c], mx.at[c], 3, sib)
     remote(bord.at[0], bc.at[c], 4, sib)
     remote(fac, fv.at[c], 5, sib)
+    remote(rs.at[0, :, rows(c, 128)], r2.at[rows(c, 128)], 17, sib)
 
     own[0].wait()
     own[4].wait()
@@ -134,6 +136,8 @@
             ftlo[at] = lo.T
     own[3].wait()
     arrived(rfs.at[oc], 2)
+    own[5].wait()
+    arrived(r2.at[rows(oc, 128)], 17)
     cr[s] = psend[s]
     arrived(psend.at[pl.ds(0, 31)], 7)
     total = cr[0].astype(F32)
@@ -150,9 +154,9 @@
         h += jnp.dot(flo[r], rh[...], preferred_element_type=F32)
         hp[pl.ds(i * 4, 4)] = h.reshape(4, 32, 128)
     for p in chips:
-        remote(hp.at[p], dr.at[q], 9, (s, p * 2 + c))
-    dr[q] = hp[q]
-    arrived(dr.at[pl.ds(0, 7)], 9)
+        remote(hp.at[p], dr.at[q], 9, (s, p * 2 + oc))
+    remote(hp.at[q], dr.at[q], 9, sib)
+    arrived(dr, 9)
     total = dr[0]
     for i in range(1, CHIPS):
         total += dr[i]
@@ -202,8 +206,8 @@
     fr[q] = fs[q]
 
     arrived(hx, 13)
-    o1v[:, rows(c, 128)] = hh[rows(c, 512)].astype(F32)
-    o1v[:, rows(oc, 128)] = hx[...].astype(F32)
+    o1v[:, rows(oc, 128)] = hh[rows(c, 512)].astype(F32)
+    o1v[:, rows(c, 128)] = hx[...].astype(F32)
     out1 = pltpu.make_async_copy(o1v, o1, loc.at[5])
     out1.start()
 
@@ -211,14 +215,14 @@
     total = fr[0].astype(F32)
     for i in range(1, CHIPS):
         total += fr[i].astype(F32)
-    ug[rows(q, 256)] = (ra[rows(q, 256)].astype(F32) - total).astype(BF)
+    ug[rows(q, 256)] = (r2[...].astype(F32) - total).astype(BF)
     for p in chips:
         remote(ug.at[rows(q, 256)], ug.at[rows(q, 256)], 15, (s, p * 2 + c))
     arrived(ug.at[pl.ds(0, 7 * 256)], 15)
     sv[...] = jnp.dot(kc[rows(oc, 128)], ug[...], preferred_element_type=F32)
-    remote(sv, o2.at[0, :, rows(c, 128)], 16, sib)
+    remote(sv, o2.at[0, :, rows(oc, 128)], 16, sib)
     o2v[...] = jnp.dot(kc[rows(c, 128)], ug[...], preferred_element_type=F32)
-    out2 = pltpu.make_async_copy(o2v, o2.at[0, :, rows(c, 128)], loc.at[6])
+    out2 = pltpu.make_async_copy(o2v, o2.at[0, :, rows(oc, 128)], loc.at[6])
     out2.start()
     arrived(sv, 16)
 
@@ -231,7 +235,7 @@
     sent(wb.at[pl.ds(0, 7 * 256)], 6)
     sent(psend.at[pl.ds(0, 31)], 7)
     sent(rh.at[pl.ds(0, 31 * 32)], 8)
-    sent(hp.at[pl.ds(0, 7)], 9)
+    sent(hp, 9)
     sent(hf.at[pl.ds(0, 7)], 10)
     sent(pf.at[pl.ds(0, 31)], 11)
     sent(hh.at[pl.ds(0, 31 * 32)], 12)
@@ -239,6 +243,7 @@
     sent(fs.at[pl.ds(0, 7)], 14)
     sent(ug.at[pl.ds(0, 7 * 256)], 15)
     sent(sv, 16)
+    sent(r2.at[rows(c, 128)], 17)
     out1.wait()
     out2.wait()
 
@@ -265,6 +270,7 @@
             pltpu.VMEM((2, 32, 128), F32),
             pltpu.VMEM((2, 32, 128), F32),
             pltpu.VMEM((2048, 128), BF),
+            pltpu.VMEM((256, 128), BF),
             pltpu.VMEM((2048, 128), BF),
             pltpu.VMEM((32, 32, 128), BF),
             pltpu.VMEM((32, 32, 128), BF),
@@ -283,9 +289,9 @@
             pltpu.VMEM((512, 256), F32),
             pltpu.VMEM((128, 128), F32),
             pltpu.VMEM((512, 128), BF),
-            pltpu.SemaphoreType.DMA((7,)),
-            pltpu.SemaphoreType.DMA((17,)),
-            pltpu.SemaphoreType.DMA((17,)),
+            pltpu.SemaphoreType.DMA((8,)),
+            pltpu.SemaphoreType.DMA((18,)),
+            pltpu.SemaphoreType.DMA((18,)),
         ],
         compiler_params=pltpu.CompilerParams(
             collective_id=0, has_side_effects=True, vmem_limit_bytes=53 << 20

time: 101 us -> 103 us (1.020)
  Pallas kernels: 97.2 us -> 99.5 us
    pallas_call x1, Pallas kernels: 97.2 us -> 99.5 us  [per_device(): pl.pallas_call(kernel, out_shape=(jax.ShapeDtypeStruct((512, 256), F32),...]
where the time goes in v4:
time: 103 us
  Pallas kernels  99.5 us (97%)
  local copies, waits for them, and re-layouts  2.94 us (3%)
    pallas_call x1, Pallas kernels, per_device(): pl.pallas_call(kernel, out_shape=(jax.ShapeDtypeStruct((512, 256), F32),...  99.5 us
    unnamed x6, local copies, waits for them, and re-layouts  2.94 us

profile of v4, /device:TPU:1, one launch (start us, length us, event | category | flops | bytes accessed | tf_op | source)
XLA Modules:
  0.0 103.1 jit_solution(10159252347247784561)
XLA Ops:
  0.6 0.0 copy-start
  0.6 0.8 copy-done
  1.5 0.0 copy-start.1
  1.5 0.7 copy-done.1
  2.1 99.5 %shard_map.77 = (f32[512,256]{1,0:T(8,128)S(1)}, f32[1,128,256]{2,1,0:T(8,128)S(1)}) custom-call(f32[512,256]{1,0:T(8,128)} %rf.1, bf16[1,128,256]{2,1,0:T(8,128)(2,1)S(1)} %copy-done, bf16[1,128,2048]{2,1,0:T(8,128)(2,1)} %kinv.1, bf16[1,2048,512]{2,1,0:T(8,128)(2,1)} %bord.1, s32[1,4]{1,0:T(1,128)S(1)} %copy-done.1, f32[256,512]{1,0:T(8,128)} %fac.1), custom_call_target="tpu_custom_call" | custom-call | flops 3000000000 | bytes 8388608 | tf_op jit(solution)/shard_map/pallas_call | solution.py:253
  101.6 0.8 copy.10
  102.4 0.7 copy.11
Async XLA Ops:
  0.6 0.8 copy-start
  1.5 0.7 copy-start.1

commit v5 on v3

--- a/solution.py
+++ b/solution.py
@@ -12,7 +12,7 @@
 HALF = 128
 Y_ORDER = (4, 3, 5, 2, 6, 1, 7, 0)
 Z_ORDER = (2, 1, 3, 0)
-SCEN_STEPS = [(dy, dz) for dy in Y_ORDER for dz in Z_ORDER if dy or dz]
+SCEN_STEPS = [(dy, dz) for dz in Z_ORDER for dy in Y_ORDER if dy or dz]
 CHIP_STEPS = [(2, 1), (1, 1), (3, 1), (2, 0), (1, 0), (3, 0), (0, 1)]
 
 

time: 101 us -> 98.9 us (0.979)
  Pallas kernels: 97.2 us -> 95.2 us
    pallas_call x1, Pallas kernels: 97.2 us -> 95.2 us  [per_device(): pl.pallas_call(kernel, out_shape=(jax.ShapeDtypeStruct((512, 256), F32),...]
where the time goes in v5:
time: 98.9 us; the launch traced here: 98.7 us
  Pallas kernels  95.2 us (96%)
  local copies, waits for them, and re-layouts  2.94 us (3%)
    pallas_call x1, Pallas kernels, per_device(): pl.pallas_call(kernel, out_shape=(jax.ShapeDtypeStruct((512, 256), F32),...  95.2 us
    unnamed x6, local copies, waits for them, and re-layouts  2.94 us

profile of v5, /device:TPU:1, one launch (start us, length us, event | category | flops | bytes accessed | tf_op | source)
XLA Modules:
  0.0 98.7 jit_solution(9967096097119521670)
XLA Ops:
  0.6 0.0 copy-start
  0.6 0.8 copy-done
  1.5 0.0 copy-start.1
  1.5 0.7 copy-done.1
  2.1 95.2 %shard_map.77 = (f32[512,256]{1,0:T(8,128)S(1)}, f32[1,128,256]{2,1,0:T(8,128)S(1)}) custom-call(f32[512,256]{1,0:T(8,128)} %rf.1, bf16[1,128,256]{2,1,0:T(8,128)(2,1)S(1)} %copy-done, bf16[1,128,2048]{2,1,0:T(8,128)(2,1)} %kinv.1, bf16[1,2048,512]{2,1,0:T(8,128)(2,1)} %bord.1, s32[1,4]{1,0:T(1,128)S(1)} %copy-done.1, f32[256,512]{1,0:T(8,128)} %fac.1), custom_call_target="tpu_custom_call" | custom-call | flops 3000000000 | bytes 8388608 | tf_op jit(solution)/shard_map/pallas_call | solution.py:248
  97.3 0.8 copy.10
  98.1 0.7 copy.11
Async XLA Ops:
  0.6 0.8 copy-start
  1.5 0.7 copy-start.1

commit v6 on v5

--- a/solution.py
+++ b/solution.py
@@ -106,14 +106,14 @@
                 bt[pl.ds(cc * 512 + j * 256, 256), rows(i, 256)] = blk.T
 
     arrived(wb.at[pl.ds(0, 7 * 256)], 6)
-    for k in range(4):
+    for k in (2, 1, 3, 0):
         r = (s // 8 + k) % 4
         p = jnp.dot(bt[rows(r, 256)], wb[...], preferred_element_type=F32)
         for j in range(2):
             keep = mx[r // 2, pl.ds(pl.multiple_of((r % 2) * 16 + j * 8, 8), 1)]
             v = jnp.where(keep > 0.5, p[j * 128 : (j + 1) * 128], 0.0)
             psend[pl.ds(r * 8 + j * 4, 4)] = v.astype(BF).reshape(4, 32, 128)
-        for j in range(8):
+        for j in (2, 6, 1, 5, 3, 7, 4, 0):
             d = r * 8 + (s % 8 + j) % 8
 
             @pl.when(d != s)
@@ -164,13 +164,13 @@
     half = hf[...].reshape(256, HALF)
     hhi = half.astype(BF)
     hlo = (half - hhi.astype(F32)).astype(BF)
-    for k in range(4):
+    for k in (2, 1, 3, 0):
         r = (s // 8 + k) % 4
         v = jnp.dot(fthi[rows(r, 256)], hhi, preferred_element_type=F32)
         v += jnp.dot(fthi[rows(r, 256)], hlo, preferred_element_type=F32)
         v += jnp.dot(ftlo[rows(r, 256)], hhi, preferred_element_type=F32)
         pf[pl.ds(r * 8, 8)] = v.astype(BF).reshape(8, 32, 128)
-        for j in range(8):
+        for j in (2, 6, 1, 5, 3, 7, 4, 0):
             d = r * 8 + (s % 8 + j) % 8
 
             @pl.when(d != s)

time: 98.9 us -> 98.1 us (level)
  no operation moved by 1% of the time
where the time goes in v6:
time: 98.1 us; the launch traced here: 97.9 us
  Pallas kernels  94.3 us (96%)
  local copies, waits for them, and re-layouts  2.94 us (3%)
    pallas_call x1, Pallas kernels, per_device(): pl.pallas_call(kernel, out_shape=(jax.ShapeDtypeStruct((512, 256), F32),...  94.3 us
    unnamed x6, local copies, waits for them, and re-layouts  2.94 us

profile of v6, /device:TPU:1, one launch (start us, length us, event | category | flops | bytes accessed | tf_op | source)
XLA Modules:
  0.0 97.9 jit_solution(18057844293125758370)
XLA Ops:
  0.6 0.0 copy-start
  0.6 0.8 copy-done
  1.5 0.0 copy-start.1
  1.5 0.7 copy-done.1
  2.1 94.3 %shard_map.77 = (f32[512,256]{1,0:T(8,128)S(1)}, f32[1,128,256]{2,1,0:T(8,128)S(1)}) custom-call(f32[512,256]{1,0:T(8,128)} %rf.1, bf16[1,128,256]{2,1,0:T(8,128)(2,1)S(1)} %copy-done, bf16[1,128,2048]{2,1,0:T(8,128)(2,1)} %kinv.1, bf16[1,2048,512]{2,1,0:T(8,128)(2,1)} %bord.1, s32[1,4]{1,0:T(1,128)S(1)} %copy-done.1, f32[256,512]{1,0:T(8,128)} %fac.1), custom_call_target="tpu_custom_call" | custom-call | flops 3000000000 | bytes 8388608 | tf_op jit(solution)/shard_map/pallas_call | solution.py:248
  96.5 0.8 copy.10
  97.3 0.7 copy.11
Async XLA Ops:
  0.6 0.8 copy-start
  1.5 0.7 copy-start.1
